TPU v7x, 512 devices: a whole 4x8x8 slice. The times are simulated.
512 devices in a mesh: slab: 128 (over y, z, core), grp: 4 (over x).
Axes of the slice: x: 4, y: 8, z: 8, core: 2. Of those that a mesh axis runs over, the one named last changes fastest.
Arguments:
- u_now: float32 [3, 2048, 32, 128], P(None, 'slab', 'grp'), may hold values from -6 to 6
- u_prev: float32 [3, 2048, 32, 128], P(None, 'slab', 'grp'), may hold values from -6 to 6
- force: float32 [3, 2048, 32, 128], P(None, 'slab', 'grp'), may hold values from -6 to 6
- stiffness: float32 [2048, 32, 128], P('slab', 'grp'), may hold values from 0.5 to 2
- broken: int32 [512, 8, 32], P('slab', 'grp'), may hold values 0 or 1
- flags: int32 [512, 8, 32], P('slab', 'grp'), may hold values 0 or 1
Outputs:
- displacement: float32 [3, 2048, 32, 128], P(None, 'slab', 'grp')
- coeffs: float32 [6, 32, 128, 2048], P(None, 'grp', 'slab')
All inputs are finite; a program needn't handle non-finite values. No bound on the sum of `broken` or of `flags` on one device may be relied on, other than what follows from the above.
Results may differ from a plain program's by a relative error of at most 0.0001.
Values sent between devices are 32-bit elements; how exact they have to be, the bound alone decides.
No kernel may reach another device: no remote copies, remote signals or barrier semaphores. Data moves between devices by JAX's collectives and lax.ppermute only.
A program may use at most 64 MiB of HBM per device.

v0:
```python
import jax
import jax.numpy as jnp
import numpy as np
from jax import lax
from jax.sharding import PartitionSpec as P

STEPS = 2
ITERS = 2
LEVELS = 3
SPRING_NORMAL = 1.0
SPRING_SHEAR = 0.4
MASS_TERM = 1.0
CRACK_CUT = 0.9


def with_halo(block, sides, width):
    for axis, dim in sides:
        count = lax.axis_size(axis)
        forward = [(i, i + 1) for i in range(count - 1)]
        backward = [(target, source) for source, target in forward]
        low = lax.ppermute(
            lax.slice_in_dim(block, block.shape[dim] - width, None, axis=dim), axis, forward
        )
        high = lax.ppermute(lax.slice_in_dim(block, 0, width, axis=dim), axis, backward)
        block = jnp.concatenate([low, block, high], axis=dim)
    return block


def cosine_table():
    freq = np.arange(4)[:, None]
    place = np.arange(4)[None, :]
    factor = np.where(freq == 0, 0.5, np.sqrt(0.5))
    return factor * np.cos(np.pi * (2 * place + 1) * freq / 8.0)


def block_table(count):
    return jnp.asarray(np.kron(np.eye(count // 4), cosine_table()), jnp.float32)


def spread(mask):
    values = mask.astype(jnp.float32)
    size_a, size_b, size_c = values.shape
    wide = jnp.broadcast_to(values[:, None, :, None, :, None], (size_a, 4, size_b, 4, size_c, 4))
    return wide.reshape(size_a * 4, size_b * 4, size_c * 4)


def sides(padded, axis_index):
    leading = padded.ndim - 3

    def cut(offset):
        index_list = [slice(None)] * leading + [slice(1, -1)] * 3
        length = padded.shape[leading + axis_index]
        index_list[leading + axis_index] = slice(1 + offset, length - 1 + offset)
        return padded[tuple(index_list)]

    return (cut(1), cut(-1))


def springs(field, weight, field_pad, weight_pad):
    result = MASS_TERM * field
    for axis_index in range(3):
        upper_v, lower_v = sides(field_pad, axis_index)
        upper_w, lower_w = sides(weight_pad, axis_index)
        k_upper = 0.5 * (weight + upper_w)
        k_lower = 0.5 * (weight + lower_w)
        change = k_upper * (field - upper_v) + k_lower * (field - lower_v)
        coupling = jnp.array(
            [SPRING_NORMAL if comp == axis_index else SPRING_SHEAR for comp in range(3)],
            jnp.float32,
        ).reshape(3, 1, 1, 1)
        result = result + coupling * change
    return result


def faces(field):
    padded = with_halo(field, (("slab", 1), ("grp", 2)), 1)
    return jnp.pad(padded, ((0, 0), (0, 0), (0, 0), (1, 1)))


def stresses(carry, field_pad):
    rows_out = []
    for axis_index in range(3):
        upper_v, lower_v = sides(field_pad, axis_index)
        rows_out.append(SPRING_NORMAL * carry * 0.5 * (upper_v[axis_index] - lower_v[axis_index]))
    return jnp.stack(rows_out)


def single_sum(value):
    return lax.psum(value, ("slab", "grp"))


def lift(signal):
    even = signal[..., 0::2]
    odd = signal[..., 1::2]
    detail = odd - 0.5 * (even + jnp.roll(even, -1, axis=-1))
    approx = even + 0.25 * (jnp.roll(detail, 1, axis=-1) + detail)
    return (approx, detail)


def wavelet(signal):
    pieces = []
    approx = signal
    for level_index in range(LEVELS):
        approx, detail = lift(approx)
        pieces.insert(0, detail)
    return jnp.concatenate([approx] + pieces, axis=-1)


def body(u_now, u_prev, force, stiffness, broken, flags):
    weight = stiffness * (1.0 - CRACK_CUT * spread(broken))
    carry = spread(flags) * weight
    weight_pad = with_halo(weight, (("slab", 0), ("grp", 1)), 1)
    weight_pad = jnp.pad(weight_pad, ((0, 0), (0, 0), (1, 1)))

    def operate(field):
        return springs(field, weight, faces(field), weight_pad)

    for step_index in range(STEPS):
        rhs = MASS_TERM * (2.0 * u_now - u_prev) + force
        guess = u_now
        residual = rhs - operate(guess)
        direction = residual
        norm_now = single_sum(jnp.sum(residual * residual))
        for turn_index in range(ITERS):
            image = operate(direction)
            alpha = norm_now / single_sum(jnp.sum(direction * image))
            guess = guess + alpha * direction
            residual = residual - alpha * image
            if turn_index + 1 < ITERS:
                norm_next = single_sum(jnp.sum(residual * residual))
                direction = residual + norm_next / norm_now * direction
                norm_now = norm_next
        u_prev = u_now
        u_now = guess
    stress = stresses(carry, faces(u_now))
    fields = jnp.concatenate([u_now, stress], axis=0)
    table_x = block_table(fields.shape[1])
    table_y = block_table(fields.shape[2])
    table_z = block_table(fields.shape[3])
    blockc = jnp.einsum("ax,hxyz->hayz", table_x, fields, precision=lax.Precision.HIGHEST)
    blockc = jnp.einsum("by,hxyz->hxbz", table_y, blockc, precision=lax.Precision.HIGHEST)
    blockc = jnp.einsum("hxyz,cz->hxyc", blockc, table_z, precision=lax.Precision.HIGHEST)
    moved = jnp.transpose(blockc, (0, 2, 3, 1))
    shipped = lax.all_to_all(moved, "slab", split_axis=2, concat_axis=3, tiled=True)
    coeffs = wavelet(shipped)
    return (u_now, coeffs)


def solution(mesh):
    return jax.shard_map(
        body,
        mesh=mesh,
        in_specs=(
            P(None, "slab", "grp", None),
            P(None, "slab", "grp", None),
            P(None, "slab", "grp", None),
            P("slab", "grp", None),
            P("slab", "grp", None),
            P("slab", "grp", None),
        ),
        out_specs=(P(None, "slab", "grp", None), P(None, "grp", "slab", None)),
        check_vma=False,
    )
```

profile of v0, /device:TPU:1, one launch (start us, length us, event | category | flops | bytes accessed | tf_op | source)
XLA Modules:
  0.0 816.2 jit_solution(5298064619461524530)
XLA Ops:
  1.8 1.6 sub.166
  3.5 5.4 collective-permute-start.2
  8.9 4.7 collective-permute-start
  13.6 1.9 collective-permute-start.1
  15.5 3.6 collective-permute-start.3
  20.5 1.3 collective-permute-start.4
  21.9 4.0 collective-permute-start.7
  25.9 1.3 collective-permute-start.5
  27.5 3.4 collective-permute-done.5
  31.6 3.8 collective-permute-start.9
  35.4 1.9 collective-permute-start.8
  37.3 3.1 collective-permute-done.8
  40.4 3.1 collective-permute-start.11
  43.5 1.3 collective-permute-start.10
  44.8 3.4 collective-permute-done.10
  49.5 106.3 %all-reduce.9 = (f32[]{:T(128)}, f32[]{:T(128)}) all-reduce(f32[]{:T(128)} %get-tuple-element.11, f32[]{:T(128)} %get-tuple-element.10), channel_id=1, replica_groups=mesh['slab'=128,'grp'=4] {'slab','grp'}, use_global_device_ids=true, to_apply=%region_1.2 | all-reduce | flops 2 | bytes 16 | tf_op jit(solution)/shard_map/psum | solution.py:89
  157.7 95.6 %psum.58 = f32[]{:T(128)} all-reduce(f32[]{:T(128)} %multiply_reduce_fusion.3), channel_id=1, replica_groups=mesh['slab'=128,'grp'=4] {'slab','grp'}, use_global_device_ids=true, to_apply=%region_5.6 | all-reduce | flops 1 | bytes 8 | tf_op jit(solution)/shard_map/psum | solution.py:89
  254.8 2.2 collective-permute-start.13
  257.0 2.1 collective-permute-start.12
  259.1 2.9 collective-permute-done.12
  262.0 2.8 collective-permute-start.15
  264.8 1.3 collective-permute-start.14
  266.1 3.4 collective-permute-done.14
  270.7 100.4 %psum.59 = f32[]{:T(128)} all-reduce(f32[]{:T(128)} %fusion.75), channel_id=1, replica_groups=mesh['slab'=128,'grp'=4] {'slab','grp'}, use_global_device_ids=true, to_apply=%region_7.8 | all-reduce | flops 1 | bytes 8 | tf_op jit(solution)/shard_map/psum | solution.py:89
  372.6 1.9 collective-permute-start.17
  374.5 2.4 collective-permute-start.16
  376.9 2.6 collective-permute-done.16
  379.6 3.7 collective-permute-start.19
  383.2 1.3 collective-permute-start.18
  384.6 3.4 collective-permute-done.18
  388.6 3.6 collective-permute-start.21
  392.2 1.9 collective-permute-start.20
  394.2 3.1 collective-permute-done.20
  397.3 1.4 collective-permute-start.23
  398.7 1.3 collective-permute-start.22
  400.0 3.4 collective-permute-done.22
  404.7 105.3 %all-reduce.8 = (f32[]{:T(128)}, f32[]{:T(128)}) all-reduce(f32[]{:T(128)} %get-tuple-element.9, f32[]{:T(128)} %get-tuple-element.8), channel_id=1, replica_groups=mesh['slab'=128,'grp'=4] {'slab','grp'}, use_global_device_ids=true, to_apply=%region_9.10 | all-reduce | flops 2 | bytes 16 | tf_op jit(solution)/shard_map/psum | solution.py:89
  511.9 95.4 %psum.62 = f32[]{:T(128)} all-reduce(f32[]{:T(128)} %multiply_reduce_fusion), channel_id=1, replica_groups=mesh['slab'=128,'grp'=4] {'slab','grp'}, use_global_device_ids=true, to_apply=%region_13.14 | all-reduce | flops 1 | bytes 8 | tf_op jit(solution)/shard_map/psum | solution.py:89
  608.7 2.2 collective-permute-start.25
  611.0 2.1 collective-permute-start.24
  613.1 2.9 collective-permute-done.24
  616.0 3.4 collective-permute-start.27
  619.4 1.3 collective-permute-start.26
  620.7 3.4 collective-permute-done.26
  625.4 100.4 %psum.63 = f32[]{:T(128)} all-reduce(f32[]{:T(128)} %fusion.15), channel_id=1, replica_groups=mesh['slab'=128,'grp'=4] {'slab','grp'}, use_global_device_ids=true, to_apply=%region_15.16 | all-reduce | flops 1 | bytes 8 | tf_op jit(solution)/shard_map/psum | solution.py:89
  727.2 1.9 collective-permute-start.29
  729.2 2.4 collective-permute-start.28
  731.6 2.6 collective-permute-done.28
  734.2 3.7 collective-permute-start.31
  739.6 1.6 reshape.62
  741.2 1.4 collective-permute-done.30
  745.3 2.1 copy.79
  747.4 1.9 reshape.66
  749.3 14.6 %all-to-all-start = ((f32[128,1,768]{2,1,0:T(1,128)}), f32[128,1,768]{2,1,0:T(1,128)S(1)}, u32[]{:S(2)}, u32[]{:S(2)}) async-start(f32[128,1,768]{2,1,0:T(1,128)} %reshape.66), calls=%async_computation | async-start | bytes 786432 | tf_op jit(solution)/shard_map/all_to_all | solution.py:144
  764.7 16.0 %all-to-all-done = f32[128,1,768]{2,1,0:T(1,128)S(1)} async-done(((f32[128,1,768]{2,1,0:T(1,128)}), f32[128,1,768]{2,1,0:T(1,128)S(1)}, u32[]{:S(2)}, u32[]{:S(2)}) %all-to-all-start) | async-done | bytes 393248 | tf_op jit(solution)/shard_map/all_to_all | solution.py:144
  781.1 1.6 reduce
  783.8 2.6 copy.80
  786.4 3.8 all_to_all.10
  790.1 6.7 slice.508
  796.8 6.9 slice.509
  804.1 3.3 slice.514
  807.4 3.3 slice.515
  811.0 1.7 slice.520
  812.7 1.7 slice.521
  (110 shorter events, 19.6 us)
Async XLA Ops:
  0.6 2.8 copy-start.3
  0.6 12.9 %copy-start = (f32[3,16,8,128]{3,2,1,0:T(8,128)S(1)}, f32[3,16,8,128]{3,2,1,0:T(8,128)}, u32[]{:S(2)}) copy-start(f32[3,16,8,128]{3,2,1,0:T(8,128)} %param.27) | copy-start | bytes 589828
  1.7 29.5 %copy-start.1 = (f32[3,16,8,128]{3,2,1,0:T(8,128)S(1)}, f32[3,16,8,128]{3,2,1,0:T(8,128)}, u32[]{:S(2)}) copy-start(f32[3,16,8,128]{3,2,1,0:T(8,128)} %param.29) | copy-start | bytes 589828
  1.7 29.5 %copy-start.2 = (f32[3,16,8,128]{3,2,1,0:T(8,128)S(1)}, f32[3,16,8,128]{3,2,1,0:T(8,128)}, u32[]{:S(2)}) copy-start(f32[3,16,8,128]{3,2,1,0:T(8,128)} %param.28) | copy-start | bytes 589828
  1.7 29.5 %copy-start.5 = (f32[3]{0:T(128)S(1)}, f32[3]{0:T(128)}, u32[]{:S(2)}) copy-start(f32[3]{0:T(128)} %constant.9.clone) | copy-start | bytes 40
  1.7 29.5 %copy-start.6 = (f32[3]{0:T(128)S(1)}, f32[3]{0:T(128)}, u32[]{:S(2)}) copy-start(f32[3]{0:T(128)} %constant.8.clone) | copy-start | bytes 40
  1.8 29.5 %copy-start.7 = (f32[3]{0:T(128)S(1)}, f32[3]{0:T(128)}, u32[]{:S(2)}) copy-start(f32[3]{0:T(128)} %constant.7.clone) | copy-start | bytes 40
  3.5 15.7 %collective-permute-start.2 = (f32[1,8,128]{2,0,1:T(1,128)S(1)}, f32[1,8,128]{2,0,1:T(1,128)S(1)}, u32[]{:S(2)}, u32[]{:S(2)}) collective-permute-start(f32[1,8,128]{2,0,1:T(1,128)S(1)} %get-tuple-element.59), channel_id=1, source_target_pairs={{0,4},{4,8},{8,12},{12,16},{16,20},{20,24},{24,28},{28,32},{32,36}... | collective-permute-start | bytes 12296 | tf_op jit(solution)/shard_map/ppermute | solution.py:21
  8.9 10.4 %collective-permute-start = (f32[1,8,128]{2,0,1:T(1,128)S(1)}, f32[1,8,128]{2,0,1:T(1,128)S(1)}, u32[]{:S(2)}, u32[]{:S(2)}) collective-permute-start(f32[1,8,128]{2,0,1:T(1,128)S(1)} %get-tuple-element.60), channel_id=1, source_target_pairs={{4,0},{8,4},{12,8},{16,12},{20,16},{24,20},{28,24},{32,28},{36,32}... | collective-permute-start | bytes 12296 | tf_op jit(solution)/shard_map/ppermute | solution.py:24
  13.6 8.3 %collective-permute-start.1 = (f32[3,1,8,128]{3,1,2,0:T(1,128)S(1)}, f32[3,1,8,128]{3,1,2,0:T(1,128)S(1)}, u32[]{:S(2)}, u32[]{:S(2)}) collective-permute-start(f32[3,1,8,128]{3,1,2,0:T(1,128)S(1)} %bitcast.62), channel_id=1, source_target_pairs={{4,0},{8,4},{12,8},{16,12},{20,16},{24,20},{28,24},{32,28},{36,32}... | collective-permute-start | bytes 36872 | tf_op jit(solution)/shard_map/ppermute | solution.py:24
  15.5 6.3 collective-permute-start.3
  19.2 7.9 collective-permute-start.6
  20.5 6.7 collective-permute-start.4
  21.9 5.6 collective-permute-start.7
  25.9 5.0 collective-permute-start.5
  31.6 5.7 collective-permute-start.9
  35.4 5.0 collective-permute-start.8
  40.4 4.4 collective-permute-start.11
  43.5 4.7 collective-permute-start.10
  254.8 4.3 collective-permute-start.13
  257.0 5.0 collective-permute-start.12
  262.0 4.1 collective-permute-start.15
  264.8 4.7 collective-permute-start.14
  372.6 4.3 collective-permute-start.17
  374.5 5.0 collective-permute-start.16
  379.6 5.0 collective-permute-start.19
  383.2 4.7 collective-permute-start.18
  388.6 5.5 collective-permute-start.21
  392.2 5.0 collective-permute-start.20
  397.3 2.7 collective-permute-start.23
  398.7 4.7 collective-permute-start.22
  403.8 335.4 %copy-start.10 = (s32[4,2,32]{2,1,0:T(2,128)S(1)}, s32[4,2,32]{2,1,0:T(2,128)}, u32[]{:S(2)}) copy-start(s32[4,2,32]{2,1,0:T(2,128)} %param.32) | copy-start | bytes 3076
  608.7 4.3 collective-permute-start.25
  611.0 5.0 collective-permute-start.24
  616.0 4.7 collective-permute-start.27
  619.4 4.7 collective-permute-start.26
  727.2 4.4 collective-permute-start.29
  729.2 13.9 %copy-start.8 = (f32[16,16,1,1]{1,0,3,2:T(8,128)S(1)}, f32[16,16,1,1]{1,0,3,2:T(8,128)}, u32[]{:S(2)}) copy-start(f32[16,16,1,1]{1,0,3,2:T(8,128)} %constant.59) | copy-start | bytes 3076
  729.2 5.0 collective-permute-start.28
  734.2 7.0 collective-permute-start.31
  737.9 4.7 collective-permute-start.30
  739.2 4.3 copy-start.9
  739.5 4.6 copy-start.4
  749.3 31.3 %all-to-all-start = ((f32[128,1,768]{2,1,0:T(1,128)}), f32[128,1,768]{2,1,0:T(1,128)S(1)}, u32[]{:S(2)}, u32[]{:S(2)}) async-start(f32[128,1,768]{2,1,0:T(1,128)} %reshape.66), calls=%async_computation | async-start | bytes 786432 | tf_op jit(solution)/shard_map/all_to_all | solution.py:144
where the time goes:
time: 826 us; the launch traced here: 816 us
  blocking collectives  603 us (73%)
  starting transfers between devices  92.5 us (11%)
  waiting for transfers between devices  54.8 us (7%)
  local copies, waits for them, and re-layouts  41.9 us (5%)
  other arithmetic  11.5 us (1%)
  between operations  9.84 us (1%)
    psum x6, blocking collectives, single_sum(): return lax.psum(value, ('slab', 'grp'))  603 us
    ppermute x16, starting transfers between devices, with_halo(): lax.ppermute(lax.slice_in_dim(block, block.shape[dim] - width, None, axis...  48 us
    ppermute x16, waiting for transfers between devices, with_halo(): lax.ppermute(lax.slice_in_dim(block, 0, width, axis=dim), axis, backward)  38.8 us
    ppermute x16, starting transfers between devices, with_halo(): lax.ppermute(lax.slice_in_dim(block, 0, width, axis=dim), axis, backward)  29.8 us
  transfers between devices with their start and end apart: 33, of which 14 were waited for; matrix products, arithmetic and copies ran while one was open for 0% of the time, Pallas kernels for 0%

commit v1 on v0

--- a/solution.py
+++ b/solution.py
@@ -86,7 +86,13 @@
 
 
 def single_sum(value):
-    return lax.psum(value, ("slab", "grp"))
+
+    def reach_the_signs(view):
+        for b in ("slab", "grp"):
+            view = lax.psum(view, axis_name=b)
+        return view
+
+    return reach_the_signs(value)
 
 
 def lift(signal):

time: 826 us -> 1800 us (2.18)
  blocking collectives: 603 us -> 1540 us
  starting transfers between devices: 92.5 us -> 138 us
    psum x6 -> x12, blocking collectives: 603 us -> 1540 us  [reach_the_signs(): view = lax.psum(view, axis_name=b)]
    all_to_all x1, starting transfers between devices: 14.6 us -> 55.6 us  [body(): lax.all_to_all(moved, 'slab', split_axis=2, concat_axis=3, tiled=True)]
where the time goes in v1:
time: 1800 us; the launch traced here: 1790 us
  blocking collectives  1540 us (86%)
  starting transfers between devices  138 us (8%)
  waiting for transfers between devices  48.3 us (3%)
  local copies, waits for them, and re-layouts  41.9 us (2%)
    psum x12, blocking collectives, reach_the_signs(): view = lax.psum(view, axis_name=b)  1540 us
    all_to_all x1, starting transfers between devices, body(): lax.all_to_all(moved, 'slab', split_axis=2, concat_axis=3, tiled=True)  55.6 us
    ppermute x16, starting transfers between devices, with_halo(): lax.ppermute(lax.slice_in_dim(block, block.shape[dim] - width, None, axis...  46.6 us
    ppermute x16, starting transfers between devices, with_halo(): lax.ppermute(lax.slice_in_dim(block, 0, width, axis=dim), axis, backward)  36.3 us
  transfers between devices with their start and end apart: 33, of which 14 were waited for; matrix products, arithmetic and copies ran while one was open for 0% of the time, Pallas kernels for 0%

profile of v1, /device:TPU:1, one launch (start us, length us, event | category | flops | bytes accessed | tf_op | source)
XLA Modules:
  0.0 1791.7 jit_solution(1191226999319184656)
XLA Ops:
  1.8 1.6 sub.166
  3.5 5.4 collective-permute-start.2
  8.9 4.7 collective-permute-start
  13.6 1.9 collective-permute-start.1
  15.5 3.6 collective-permute-start.3
  20.5 1.3 collective-permute-start.4
  21.9 4.0 collective-permute-start.7
  27.5 3.4 collective-permute-done.5
  31.6 3.8 collective-permute-start.9
  35.4 1.9 collective-permute-start.8
  37.3 3.1 collective-permute-done.8
  40.4 3.1 collective-permute-start.11
  43.5 1.3 collective-permute-start.10
  44.8 3.4 collective-permute-done.10
  49.5 252.7 %all-reduce.9 = (f32[]{:T(128)}, f32[]{:T(128)}) all-reduce(f32[]{:T(128)} %get-tuple-element.11, f32[]{:T(128)} %get-tuple-element.10), channel_id=1, replica_groups=mesh['slab'=128,'grp'=4] {'slab'}, use_global_device_ids=true, to_apply=%region_1.2 | all-reduce | flops 2 | bytes 16 | tf_op jit(solution)/shard_map/psum | solution.py:92
  302.2 7.5 all-reduce.11
  311.7 251.0 %psum.116 = f32[]{:T(128)} all-reduce(f32[]{:T(128)} %multiply_reduce_fusion.3), channel_id=1, replica_groups=mesh['slab'=128,'grp'=4] {'slab'}, use_global_device_ids=true, to_apply=%region_7.8 | all-reduce | flops 1 | bytes 8 | tf_op jit(solution)/shard_map/psum | solution.py:92
  562.7 7.0 psum.117
  571.1 1.9 collective-permute-start.13
  573.0 3.9 collective-permute-start.12
  578.0 3.0 collective-permute-start.15
  582.3 3.4 collective-permute-done.14
  587.0 248.3 %psum.118 = f32[]{:T(128)} all-reduce(f32[]{:T(128)} %fusion.75), channel_id=1, replica_groups=mesh['slab'=128,'grp'=4] {'slab'}, use_global_device_ids=true, to_apply=%region_10.11 | all-reduce | flops 1 | bytes 8 | tf_op jit(solution)/shard_map/psum | solution.py:92
  835.3 6.6 psum.119
  843.3 1.9 collective-permute-start.17
  845.2 3.7 collective-permute-start.16
  848.9 1.3 collective-permute-done.16
  850.3 3.4 collective-permute-start.19
  854.9 3.4 collective-permute-done.18
  859.0 3.4 collective-permute-start.21
  862.4 1.9 collective-permute-start.20
  864.3 3.1 collective-permute-done.20
  867.4 1.6 collective-permute-start.23
  869.1 1.3 collective-permute-start.22
  870.4 3.4 collective-permute-done.22
  875.0 246.3 %all-reduce.8 = (f32[]{:T(128)}, f32[]{:T(128)}) all-reduce(f32[]{:T(128)} %get-tuple-element.9, f32[]{:T(128)} %get-tuple-element.8), channel_id=1, replica_groups=mesh['slab'=128,'grp'=4] {'slab'}, use_global_device_ids=true, to_apply=%region_13.14 | all-reduce | flops 2 | bytes 16 | tf_op jit(solution)/shard_map/psum | solution.py:92
  1121.3 8.0 all-reduce.10
  1131.3 250.2 %psum.124 = f32[]{:T(128)} all-reduce(f32[]{:T(128)} %multiply_reduce_fusion), channel_id=1, replica_groups=mesh['slab'=128,'grp'=4] {'slab'}, use_global_device_ids=true, to_apply=%region_19.20 | all-reduce | flops 1 | bytes 8 | tf_op jit(solution)/shard_map/psum | solution.py:92
  1381.5 7.0 psum.125
  1389.9 1.9 collective-permute-start.25
  1391.8 3.9 collective-permute-start.24
  1396.9 3.0 collective-permute-start.27
  1401.2 3.4 collective-permute-done.26
  1405.8 248.3 %psum.126 = f32[]{:T(128)} all-reduce(f32[]{:T(128)} %fusion.15), channel_id=1, replica_groups=mesh['slab'=128,'grp'=4] {'slab'}, use_global_device_ids=true, to_apply=%region_22.23 | all-reduce | flops 1 | bytes 8 | tf_op jit(solution)/shard_map/psum | solution.py:92
  1654.1 6.6 psum.127
  1662.1 1.9 collective-permute-start.29
  1664.0 3.7 collective-permute-start.28
  1667.7 1.3 collective-permute-done.28
  1669.1 3.4 collective-permute-start.31
  1672.4 1.8 collective-permute-start.30
  1674.6 1.6 reshape.62
  1679.9 2.1 copy.79
  1682.0 1.9 reshape.66
  1683.8 55.6 %all-to-all-start = ((f32[128,1,768]{2,1,0:T(1,128)}), f32[128,1,768]{2,1,0:T(1,128)S(1)}, u32[]{:S(2)}, u32[]{:S(2)}) async-start(f32[128,1,768]{2,1,0:T(1,128)} %reshape.66), calls=%async_computation | async-start | bytes 786432 | tf_op jit(solution)/shard_map/all_to_all | solution.py:150
  1740.2 16.0 all-to-all-done
  1756.6 1.6 reduce
  1759.3 2.6 copy.80
  1761.9 3.8 all_to_all.10
  1765.7 6.7 slice.508
  1772.3 6.9 slice.509
  1779.6 3.3 slice.514
  1782.9 3.3 slice.515
  1786.6 1.7 slice.520
  1788.2 1.7 slice.521
  (116 shorter events, 26.7 us)
Async XLA Ops:
  0.6 2.8 copy-start.3
  0.6 12.9 copy-start
  1.7 29.5 %copy-start.1 = (f32[3,16,8,128]{3,2,1,0:T(8,128)S(1)}, f32[3,16,8,128]{3,2,1,0:T(8,128)}, u32[]{:S(2)}) copy-start(f32[3,16,8,128]{3,2,1,0:T(8,128)} %param.29) | copy-start | bytes 589828
  1.7 29.5 %copy-start.2 = (f32[3,16,8,128]{3,2,1,0:T(8,128)S(1)}, f32[3,16,8,128]{3,2,1,0:T(8,128)}, u32[]{:S(2)}) copy-start(f32[3,16,8,128]{3,2,1,0:T(8,128)} %param.28) | copy-start | bytes 589828
  1.7 29.5 %copy-start.5 = (f32[3]{0:T(128)S(1)}, f32[3]{0:T(128)}, u32[]{:S(2)}) copy-start(f32[3]{0:T(128)} %constant.9.clone) | copy-start | bytes 40
  1.7 29.5 %copy-start.6 = (f32[3]{0:T(128)S(1)}, f32[3]{0:T(128)}, u32[]{:S(2)}) copy-start(f32[3]{0:T(128)} %constant.8.clone) | copy-start | bytes 40
  1.8 29.5 %copy-start.7 = (f32[3]{0:T(128)S(1)}, f32[3]{0:T(128)}, u32[]{:S(2)}) copy-start(f32[3]{0:T(128)} %constant.7.clone) | copy-start | bytes 40
  3.5 15.7 collective-permute-start.2
  8.9 10.4 collective-permute-start
  13.6 8.3 collective-permute-start.1
  15.5 6.3 collective-permute-start.3
  19.2 7.9 collective-permute-start.6
  20.5 6.7 collective-permute-start.4
  21.9 5.6 collective-permute-start.7
  25.9 5.0 collective-permute-start.5
  31.6 5.7 collective-permute-start.9
  35.4 5.0 collective-permute-start.8
  40.4 4.4 collective-permute-start.11
  43.5 4.7 collective-permute-start.10
  571.1 5.8 collective-permute-start.13
  573.0 5.0 collective-permute-start.12
  578.0 4.3 collective-permute-start.15
  581.0 4.7 collective-permute-start.14
  843.3 5.6 collective-permute-start.17
  845.2 5.0 collective-permute-start.16
  850.3 4.7 collective-permute-start.19
  853.6 4.7 collective-permute-start.18
  859.0 5.3 collective-permute-start.21
  862.4 5.0 collective-permute-start.20
  867.4 3.0 collective-permute-start.23
  869.1 4.7 collective-permute-start.22
  874.1 800.1 %copy-start.10 = (s32[4,2,32]{2,1,0:T(2,128)S(1)}, s32[4,2,32]{2,1,0:T(2,128)}, u32[]{:S(2)}) copy-start(s32[4,2,32]{2,1,0:T(2,128)} %param.32) | copy-start | bytes 3076
  1389.9 5.8 collective-permute-start.25
  1391.8 5.0 collective-permute-start.24
  1396.9 4.3 collective-permute-start.27
  1399.8 4.7 collective-permute-start.26
  1662.1 5.6 collective-permute-start.29
  1664.0 13.6 copy-start.8
  1664.0 5.0 collective-permute-start.28
  1669.1 7.2 collective-permute-start.31
  1672.4 4.7 collective-permute-start.30
  1674.2 3.9 copy-start.9
  1674.6 4.1 copy-start.4
  1683.8 72.3 %all-to-all-start = ((f32[128,1,768]{2,1,0:T(1,128)}), f32[128,1,768]{2,1,0:T(1,128)S(1)}, u32[]{:S(2)}, u32[]{:S(2)}) async-start(f32[128,1,768]{2,1,0:T(1,128)} %reshape.66), calls=%async_computation | async-start | bytes 786432 | tf_op jit(solution)/shard_map/all_to_all | solution.py:150
